TPU v7x, 128 devices: a whole 4x4x4 slice. The times are simulated.
128 devices in a mesh: dp: 16 (over z, x_hi, core), tensor: 8 (over y, x_lo).
Axes of the slice: x: 4 (x_hi: 2, x_lo: 2; x = x_hi * 2 + x_lo), y: 4, z: 4, core: 2. Of those that a mesh axis runs over, the one named last changes fastest.
Arguments:
- tokens: bfloat16 [16384, 1024], P(('dp', 'tensor')), may hold values from -6 to 6
- segment_ids: int32 [16, 1024], P('dp'), may hold values from 0 to 3, never falling along the last dimension, each value on 1 to 512 neighbouring positions
- first_gain: float32 [1024], replicated, may hold values from 0.5 to 1.5
- query_gain: float32 [128], replicated, may hold values from 0.5 to 1.5
- key_gain: float32 [128], replicated, may hold values from 0.5 to 1.5
- query_weight: bfloat16 [1024, 2048], P('dp', 'tensor'), may hold values from -0.1875 to 0.1875
- key_weight: bfloat16 [1024, 1024], P('dp', 'tensor'), may hold values from -0.1875 to 0.1875
- value_weight: bfloat16 [1024, 1024], P('dp', 'tensor'), may hold values from -0.1875 to 0.1875
- out_weight: bfloat16 [2048, 1024], P('tensor', 'dp'), may hold values from -0.5 to 0.5
- second_gain: float32 [1024], replicated, may hold values from 0.5 to 1.5
- gate_weight: bfloat16 [1024, 3072], P('dp', 'tensor'), may hold values from -0.1875 to 0.1875
- up_weight: bfloat16 [1024, 3072], P('dp', 'tensor'), may hold values from -0.1875 to 0.1875
- down_weight: bfloat16 [3072, 1024], P('tensor', 'dp'), may hold values from -0.109375 to 0.109375
- cotangent: bfloat16 [16384, 1024], P(('dp', 'tensor')), may hold values from -6 to 6
Outputs:
- layer_out: bfloat16 [16384, 1024], P(('dp', 'tensor'))
- grad_tokens: bfloat16 [16384, 1024], P(('dp', 'tensor'))
- grad_first_gain: float32 [1024], replicated
- grad_query_gain: float32 [128], replicated
- grad_key_gain: float32 [128], replicated
- grad_query: float32 [1024, 2048], P('dp', 'tensor')
- grad_key: float32 [1024, 1024], P('dp', 'tensor')
- grad_value: float32 [1024, 1024], P('dp', 'tensor')
- grad_out: float32 [2048, 1024], P('tensor', 'dp')
- grad_second_gain: float32 [1024], replicated
- grad_gate: float32 [1024, 3072], P('dp', 'tensor')
- grad_up: float32 [1024, 3072], P('dp', 'tensor')
- grad_down: float32 [3072, 1024], P('tensor', 'dp')
Inputs may be any that keep to these rules, and one draw needn't show every extreme that they name: `segment_ids`: in each row, sequence numbers never fall and each sequence has 1 to 512 tokens; some sequence has exactly 512.
All inputs are finite; a program needn't handle non-finite values.
Results may differ from a plain program's by a relative error of at most 0.023.
Values may be sent and summed in bfloat16 or wider, within the bound.
No kernel may reach another device: no remote copies, remote signals or barrier semaphores. Data moves between devices by JAX's collectives and lax.ppermute only.
A program may use at most 128 MiB of HBM per device.

v0:
```python
import functools

import jax
import jax.numpy as jnp
from jax import lax
from jax.sharding import PartitionSpec as P

QBLOCK = 512


EPSILON = 1e-06
ROPE_BASE = 1000000.0
NEG_LARGE = -1e30


def norm_scale(values, weight_gain):
    return values * lax.rsqrt(jnp.mean(values * values, -1, keepdims=True) + EPSILON) * weight_gain


def rotate(values, cosine, sine):
    half_dim = values.shape[-1] // 2
    turned = jnp.concatenate([-values[..., half_dim:], values[..., :half_dim]], -1)
    return values * cosine + turned * sine


def positions_of(seg_row):
    length = seg_row.shape[0]
    indices = jnp.arange(length, dtype=jnp.int32)
    change = jnp.concatenate([jnp.ones((1,), jnp.bool_), seg_row[1:] != seg_row[:-1]])
    starts = lax.cummax(jnp.where(change, indices, 0), axis=0)
    return indices - starts


def angles_of(seg_row, head_size):
    places = positions_of(seg_row).astype(jnp.float32)
    inverse = ROPE_BASE ** (-jnp.arange(0, head_size, 2, dtype=jnp.float32) / head_size)
    phases = places[:, None] * inverse[None, :]
    phases = jnp.concatenate([phases, phases], -1)[:, None, :]
    return (jnp.cos(phases), jnp.sin(phases))


def head_prep(projected, head_gain, cosine, sine, head_count):
    shaped = projected.reshape(projected.shape[0], head_count, -1)
    return rotate(norm_scale(shaped, head_gain), cosine, sine)


def mask_of(seg_row, seg_padded, start_row, block_rows):
    seg_query = lax.dynamic_slice_in_dim(seg_row, start_row, block_rows, 0)
    seg_key = lax.dynamic_slice_in_dim(seg_padded, start_row, 2 * block_rows, 0)
    query_index = start_row + jnp.arange(block_rows, dtype=jnp.int32)
    key_index = start_row - block_rows + jnp.arange(2 * block_rows, dtype=jnp.int32)
    return (seg_query[:, None] == seg_key[None, :]) & (key_index[None, :] <= query_index[:, None])


def swiglu(gate_part, up_part):
    return jax.nn.silu(gate_part) * up_part


def dot_float(left_side, right_side):
    return jnp.dot(left_side, right_side, preferred_element_type=jnp.float32)


def per_device(
    tokens,
    segment_ids,
    first_gain,
    query_gain,
    key_gain,
    query_weight,
    key_weight,
    value_weight,
    out_weight,
    second_gain,
    gate_weight,
    up_weight,
    down_weight,
    cotangent,
):
    head_size = query_gain.shape[0]
    local_query = query_weight.shape[1] // head_size
    local_kv = key_weight.shape[1] // head_size
    group_size = local_query // local_kv
    seg_row = segment_ids[0]
    token_count = seg_row.shape[0]
    block_count = token_count // QBLOCK
    score_scale = head_size ** (-0.5)
    cosine, sine = angles_of(seg_row, head_size)
    seg_padded = jnp.concatenate([jnp.full((QBLOCK,), -1, jnp.int32), seg_row])
    gathered = (
        lax.all_gather(query_weight, "dp", axis=0, tiled=True),
        lax.all_gather(key_weight, "dp", axis=0, tiled=True),
        lax.all_gather(value_weight, "dp", axis=0, tiled=True),
        lax.all_gather(out_weight, "dp", axis=1, tiled=True),
        lax.all_gather(gate_weight, "dp", axis=0, tiled=True),
        lax.all_gather(up_weight, "dp", axis=0, tiled=True),
        lax.all_gather(down_weight, "dp", axis=1, tiled=True),
    )
    query_full, key_full, value_full, out_full, gate_full, up_full, down_full = gathered
    input_float = tokens.astype(jnp.float32)
    normed_one, first_back = jax.vjp(norm_scale, input_float, first_gain)
    normed_one_all = lax.all_gather(normed_one.astype(jnp.bfloat16), "tensor", axis=0, tiled=True)
    query_raw = dot_float(normed_one_all, query_full)
    key_raw = dot_float(normed_one_all, key_full)
    value_raw = dot_float(normed_one_all, value_full)
    query_rot, query_back = jax.vjp(
        functools.partial(head_prep, cosine=cosine, sine=sine, head_count=local_query),
        query_raw,
        query_gain,
    )
    key_rot, key_back = jax.vjp(
        functools.partial(head_prep, cosine=cosine, sine=sine, head_count=local_kv),
        key_raw,
        key_gain,
    )
    query_low = query_rot.astype(jnp.bfloat16).reshape(token_count, local_kv, group_size, head_size)
    key_low = key_rot.astype(jnp.bfloat16)
    value_low = value_raw.astype(jnp.bfloat16).reshape(token_count, local_kv, head_size)
    zero_rows = jnp.zeros((QBLOCK, local_kv, head_size), jnp.bfloat16)
    key_padded = jnp.concatenate([zero_rows, key_low], 0)
    value_padded = jnp.concatenate([zero_rows, value_low], 0)

    def window_of(start_row):
        query_block = lax.dynamic_slice_in_dim(query_low, start_row, QBLOCK, 0)
        key_block = lax.dynamic_slice_in_dim(key_padded, start_row, 2 * QBLOCK, 0)
        value_block = lax.dynamic_slice_in_dim(value_padded, start_row, 2 * QBLOCK, 0)
        allowed = mask_of(seg_row, seg_padded, start_row, QBLOCK)
        scores = (
            jnp.einsum("qhgd,khd->hgqk", query_block, key_block, preferred_element_type=jnp.float32)
            * score_scale
        )
        return (query_block, key_block, value_block, allowed, scores)

    def forward_block(block_index):
        query_block, key_block, value_block, allowed, scores = window_of(block_index * QBLOCK)
        masked = jnp.where(allowed, scores, NEG_LARGE)
        row_max = jnp.max(masked, -1, keepdims=True)
        exponent = jnp.exp(masked - row_max)
        row_total = jnp.sum(exponent, -1, keepdims=True)
        attn_prob = (exponent / row_total).astype(jnp.bfloat16)
        head_out = jnp.einsum(
            "hgqk,khd->qhgd", attn_prob, value_block, preferred_element_type=jnp.float32
        )
        return (head_out.astype(jnp.bfloat16), row_max + jnp.log(row_total))

    head_blocks, log_totals = lax.map(forward_block, jnp.arange(block_count, dtype=jnp.int32))
    attended = head_blocks.reshape(token_count, local_query * head_size)
    attn_branch = lax.psum_scatter(
        dot_float(attended, out_full).astype(jnp.bfloat16),
        "tensor",
        scatter_dimension=0,
        tiled=True,
    ).astype(jnp.float32)
    hidden_state = input_float + attn_branch
    normed_two, second_back = jax.vjp(norm_scale, hidden_state, second_gain)
    normed_two_all = lax.all_gather(normed_two.astype(jnp.bfloat16), "tensor", axis=0, tiled=True)
    gate_value = dot_float(normed_two_all, gate_full)
    up_value = dot_float(normed_two_all, up_full)
    activated, swiglu_back = jax.vjp(swiglu, gate_value, up_value)
    activated_low = activated.astype(jnp.bfloat16)
    mlp_branch = lax.psum_scatter(
        dot_float(activated_low, down_full).astype(jnp.bfloat16),
        "tensor",
        scatter_dimension=0,
        tiled=True,
    ).astype(jnp.float32)
    layer_out = (hidden_state + mlp_branch).astype(jnp.bfloat16)
    regathered = (
        lax.all_gather(query_weight, "dp", axis=0, tiled=True),
        lax.all_gather(key_weight, "dp", axis=0, tiled=True),
        lax.all_gather(value_weight, "dp", axis=0, tiled=True),
        lax.all_gather(out_weight, "dp", axis=1, tiled=True),
        lax.all_gather(gate_weight, "dp", axis=0, tiled=True),
        lax.all_gather(up_weight, "dp", axis=0, tiled=True),
        lax.all_gather(down_weight, "dp", axis=1, tiled=True),
    )
    query_full, key_full, value_full, out_full, gate_full, up_full, down_full = regathered
    cot_all = lax.all_gather(cotangent, "tensor", axis=0, tiled=True)
    grad_activated = dot_float(cot_all, down_full.T)
    grad_gate_val, grad_up_val = swiglu_back(grad_activated)
    gate_grad_low = grad_gate_val.astype(jnp.bfloat16)
    up_grad_low = grad_up_val.astype(jnp.bfloat16)
    grad_normed_two = lax.psum_scatter(
        (dot_float(gate_grad_low, gate_full.T) + dot_float(up_grad_low, up_full.T)).astype(
            jnp.bfloat16
        ),
        "tensor",
        scatter_dimension=0,
        tiled=True,
    ).astype(jnp.float32)
    grad_gate_mat = dot_float(normed_two_all.T, gate_grad_low)
    grad_up_mat = dot_float(normed_two_all.T, up_grad_low)
    grad_down_mat = dot_float(activated_low.T, cot_all)
    grad_hidden_norm, grad_second = second_back(grad_normed_two)
    grad_hidden = cotangent.astype(jnp.float32) + grad_hidden_norm
    hidden_grad_all = lax.all_gather(grad_hidden.astype(jnp.bfloat16), "tensor", axis=0, tiled=True)
    grad_attended = (
        dot_float(hidden_grad_all, out_full.T)
        .astype(jnp.bfloat16)
        .reshape(token_count, local_kv, group_size, head_size)
    )
    grad_out_mat = dot_float(attended.T, hidden_grad_all)

    def backward_block(carry, block_index):
        key_accum, value_accum = carry
        start_row = block_index * QBLOCK
        query_block, key_block, value_block, allowed, scores = window_of(start_row)
        attn_prob = jnp.where(allowed, jnp.exp(scores - log_totals[block_index]), 0.0)
        prob_low = attn_prob.astype(jnp.bfloat16)
        grad_block = lax.dynamic_slice_in_dim(grad_attended, start_row, QBLOCK, 0)
        grad_prob = jnp.einsum(
            "qhgd,khd->hgqk", grad_block, value_block, preferred_element_type=jnp.float32
        )
        inner_sum = jnp.sum(attn_prob * grad_prob, -1, keepdims=True)
        grad_scores = (attn_prob * (grad_prob - inner_sum)).astype(jnp.bfloat16)
        grad_query_part = (
            jnp.einsum("hgqk,khd->qhgd", grad_scores, key_block, preferred_element_type=jnp.float32)
            * score_scale
        )
        grad_key_part = (
            jnp.einsum(
                "hgqk,qhgd->khd", grad_scores, query_block, preferred_element_type=jnp.float32
            )
            * score_scale
        )
        grad_value_part = jnp.einsum(
            "hgqk,qhgd->khd", prob_low, grad_block, preferred_element_type=jnp.float32
        )
        key_accum = lax.dynamic_update_slice_in_dim(
            key_accum,
            lax.dynamic_slice_in_dim(key_accum, start_row, 2 * QBLOCK, 0) + grad_key_part,
            start_row,
            0,
        )
        value_accum = lax.dynamic_update_slice_in_dim(
            value_accum,
            lax.dynamic_slice_in_dim(value_accum, start_row, 2 * QBLOCK, 0) + grad_value_part,
            start_row,
            0,
        )
        return ((key_accum, value_accum), grad_query_part)

    accum_zeros = jnp.zeros((token_count + QBLOCK, local_kv, head_size), jnp.float32)
    final_carry, query_blocks = lax.scan(
        backward_block, (accum_zeros, accum_zeros), jnp.arange(block_count, dtype=jnp.int32)
    )
    key_accum, value_accum = final_carry
    grad_query_raw, grad_query_gain = query_back(
        query_blocks.reshape(token_count, local_query, head_size)
    )
    grad_key_raw, grad_key_gain = key_back(key_accum[QBLOCK:])
    query_grad_low = grad_query_raw.astype(jnp.bfloat16)
    key_grad_low = grad_key_raw.astype(jnp.bfloat16)
    value_grad_low = (
        value_accum[QBLOCK:].reshape(token_count, local_kv * head_size).astype(jnp.bfloat16)
    )
    grad_normed_one = lax.psum_scatter(
        (
            dot_float(query_grad_low, query_full.T)
            + dot_float(key_grad_low, key_full.T)
            + dot_float(value_grad_low, value_full.T)
        ).astype(jnp.bfloat16),
        "tensor",
        scatter_dimension=0,
        tiled=True,
    ).astype(jnp.float32)
    grad_query_mat = dot_float(normed_one_all.T, query_grad_low)
    grad_key_mat = dot_float(normed_one_all.T, key_grad_low)
    grad_value_mat = dot_float(normed_one_all.T, value_grad_low)
    grad_input_norm, grad_first = first_back(grad_normed_one)
    grad_tokens = (grad_hidden + grad_input_norm).astype(jnp.bfloat16)
    owned = (
        lax.psum_scatter(
            grad_query_mat.astype(jnp.bfloat16), "dp", scatter_dimension=0, tiled=True
        ).astype(jnp.float32),
        lax.psum_scatter(
            grad_key_mat.astype(jnp.bfloat16), "dp", scatter_dimension=0, tiled=True
        ).astype(jnp.float32),
        lax.psum_scatter(
            grad_value_mat.astype(jnp.bfloat16), "dp", scatter_dimension=0, tiled=True
        ).astype(jnp.float32),
        lax.psum_scatter(
            grad_out_mat.astype(jnp.bfloat16), "dp", scatter_dimension=1, tiled=True
        ).astype(jnp.float32),
        lax.psum_scatter(
            grad_gate_mat.astype(jnp.bfloat16), "dp", scatter_dimension=0, tiled=True
        ).astype(jnp.float32),
        lax.psum_scatter(
            grad_up_mat.astype(jnp.bfloat16), "dp", scatter_dimension=0, tiled=True
        ).astype(jnp.float32),
        lax.psum_scatter(
            grad_down_mat.astype(jnp.bfloat16), "dp", scatter_dimension=1, tiled=True
        ).astype(jnp.float32),
    )
    gain_sums = lax.psum(
        (grad_first, grad_query_gain, grad_key_gain, grad_second), ("dp", "tensor")
    )
    return (
        layer_out,
        grad_tokens,
        gain_sums[0],
        gain_sums[1],
        gain_sums[2],
        owned[0],
        owned[1],
        owned[2],
        owned[3],
        gain_sums[3],
        owned[4],
        owned[5],
        owned[6],
    )


def solution(mesh):
    in_specs = (
        P(("dp", "tensor"), None),
        P("dp", None),
        P(),
        P(),
        P(),
        P("dp", "tensor"),
        P("dp", "tensor"),
        P("dp", "tensor"),
        P("tensor", "dp"),
        P(),
        P("dp", "tensor"),
        P("dp", "tensor"),
        P("tensor", "dp"),
        P(("dp", "tensor"), None),
    )
    out_specs = (
        P(("dp", "tensor"), None),
        P(("dp", "tensor"), None),
        P(),
        P(),
        P(),
        P("dp", "tensor"),
        P("dp", "tensor"),
        P("dp", "tensor"),
        P("tensor", "dp"),
        P(),
        P("dp", "tensor"),
        P("dp", "tensor"),
        P("tensor", "dp"),
    )
    return jax.shard_map(
        per_device, mesh=mesh, in_specs=in_specs, out_specs=out_specs, check_vma=False
    )
```

profile of v0, /device:TPU:1, one launch (start us, length us, event | category | flops | bytes accessed | tf_op | source)
XLA Modules:
  0.0 1062.6 jit_solution(13979652074072549132)
XLA Ops:
  12.4 29.3 %all_gather.42 = bf16[1024,128]{1,0:T(8,128)(2,1)S(1)} all-gather(bf16[64,128]{1,0:T(8,128)(2,1)} %param.24), channel_id=1, replica_groups=mesh['dp'=16,'tensor'=8] {'dp'}, dimensions={0}, use_global_device_ids=true | all-gather | bytes 278528 | tf_op jit(solution)/shard_map/all_gather | solution.py:91
  41.7 22.4 %all_gather.41 = bf16[1024,128]{1,0:T(8,128)(2,1)S(1)} all-gather(bf16[64,128]{1,0:T(8,128)(2,1)} %param.25), channel_id=1, replica_groups=mesh['dp'=16,'tensor'=8] {'dp'}, dimensions={0}, use_global_device_ids=true | all-gather | bytes 278528 | tf_op jit(solution)/shard_map/all_gather | solution.py:92
  65.1 24.0 %all_gather.43 = bf16[1024,256]{1,0:T(8,128)(2,1)S(1)} all-gather(bf16[64,256]{1,0:T(8,128)(2,1)S(1)} %copy-done.45), channel_id=1, replica_groups=mesh['dp'=16,'tensor'=8] {'dp'}, dimensions={0}, use_global_device_ids=true | all-gather | bytes 557056 | tf_op jit(solution)/shard_map/all_gather | solution.py:90
  89.1 23.3 %all_gather.44 = bf16[256,1024]{0,1:T(8,128)(2,1)} all-gather(bf16[256,64]{0,1:T(8,128)(2,1)S(1)} %copy-done.46), channel_id=1, replica_groups=mesh['dp'=16,'tensor'=8] {'dp'}, dimensions={1}, use_global_device_ids=true | all-gather | bytes 557056 | tf_op jit(solution)/shard_map/all_gather | solution.py:93
  135.3 18.5 %while.30 = (s32[]{:T(128)}, bf16[2,512,1,2,128]{4,3,1,0,2:T(2,128)(2,1)}, f32[2,1,2,512,1]{3,2,4,1,0:T(2,128)}, s32[2]{0:T(128)S(1)}, bf16[1536,1,128]{2,0,1:T(...) while((s32[]{:T(128)}, ...), condition=%wide.region_8.9_spmd, body=%wide.region_5.8_spmd.sunk | while | flops 551158272 | bytes 16840984 | solution.py:145
  153.9 3.2 convolution_convert_fusion.1
  157.1 52.1 %reduce-scatter.12.cloned.1.call-done = bf16[128,1024]{1,0:T(8,128)(2,1)} async-done(((bf16[1024,1024]{1,0:T(8,128)(2,1)}), bf16[128,1024]{1,0:T(8,128)(2,1)}) %reduce-scatter.12.cloned.1.call-update) | async-done | bytes 262160 | tf_op jit(solution)/shard_map/reduce_scatter | solution.py:147
  212.9 35.9 %all_gather.46 = bf16[1024,384]{1,0:T(8,128)(2,1)S(1)} all-gather(bf16[64,384]{1,0:T(8,128)(2,1)} %param.28), channel_id=1, replica_groups=mesh['dp'=16,'tensor'=8] {'dp'}, dimensions={0}, use_global_device_ids=true | all-gather | bytes 835584 | tf_op jit(solution)/shard_map/all_gather | solution.py:94
  248.8 31.2 %all_gather.47 = bf16[1024,384]{1,0:T(8,128)(2,1)} all-gather(bf16[64,384]{1,0:T(8,128)(2,1)} %param.29), channel_id=1, replica_groups=mesh['dp'=16,'tensor'=8] {'dp'}, dimensions={0}, use_global_device_ids=true | all-gather | bytes 835584 | tf_op jit(solution)/shard_map/all_gather | solution.py:95
  280.0 33.0 %all_gather.48 = bf16[384,1024]{0,1:T(8,128)(2,1)} all-gather(bf16[384,64]{0,1:T(8,128)(2,1)} %param.30), channel_id=1, replica_groups=mesh['dp'=16,'tensor'=8] {'dp'}, dimensions={1}, use_global_device_ids=true | all-gather | bytes 835584 | tf_op jit(solution)/shard_map/all_gather | solution.py:96
  313.0 4.3 fusion.125
  319.7 12.6 %all-gather.9.cloned.1.call-done = bf16[1024,1024]{1,0:T(8,128)(2,1)} async-done(((bf16[128,1024]{1,0:T(8,128)(2,1)}), bf16[1024,1024]{1,0:T(8,128)(2,1)}) %all-gather.9.cloned.1.call-update) | async-done | bytes 2097168 | tf_op jit(solution)/shard_map/all_gather | solution.py:177
  332.4 5.5 multiply_convert_fusion
  342.3 52.2 %reduce-scatter.16.cloned.1.call-done = bf16[128,1024]{1,0:T(8,128)(2,1)} async-done(((bf16[1024,1024]{1,0:T(8,128)(2,1)}), bf16[128,1024]{1,0:T(8,128)(2,1)}) %reduce-scatter.16.cloned.1.call-update) | async-done | bytes 262160 | tf_op jit(solution)/shard_map/reduce_scatter | solution.py:182
  398.3 4.0 convolution_convert_fusion.2
  402.4 4.0 convolution_convert_fusion.3
  406.5 3.8 convolution_convert_fusion.4
  410.6 39.1 %all-gather.11.cloned.1.call-done = bf16[1024,1024]{1,0:T(8,128)(2,1)} async-done(((bf16[128,1024]{1,0:T(8,128)(2,1)}), bf16[1024,1024]{1,0:T(8,128)(2,1)}) %all-gather.11.cloned.1.call-update) | async-done | bytes 2097168 | tf_op jit(solution)/shard_map/all_gather | solution.py:195
  449.7 3.2 convolution_convert_fusion.7
  455.4 36.9 %while.31 = (s32[]{:T(128)}, f32[1536,1,128]{0,2,1:T(8,128)}, f32[1536,1,128]{0,2,1:T(8,128)}, f32[2,512,1,2,128]{4,1,0,3,2:T(8,128)}, s32[2]{0:T(128)}, /*index...) while((s32[]{:T(128)}, f32[1536,1,128]{0,2,1:T(8,128)}, ...), condition=%wide.region_16.17_spmd, body=%wide.region_14.16_spmd.sunk | while | flops 1360003584 | bytes 40167792 | solution.py:243
  462.6 3.2 fusion.205
  481.1 3.2 fusion.205
  505.9 3.8 multiply_reduce_fusion
  521.9 3.1 add_convert_fusion
  530.7 56.1 %reduce-scatter.30.cloned.1.call-done = bf16[64,384]{1,0:T(8,128)(2,1)} async-done(((bf16[1024,384]{1,0:T(8,128)(2,1)}), bf16[64,384]{1,0:T(8,128)(2,1)}) %reduce-scatter.30.cloned.1.call-update) | async-done | bytes 49168 | tf_op jit(solution)/shard_map/reduce_scatter | solution.py:287
  588.3 67.5 %reduce-scatter.28.cloned.1.call-done = bf16[64,384]{1,0:T(8,128)(2,1)} async-done(((bf16[1024,384]{1,0:T(8,128)(2,1)}), bf16[64,384]{1,0:T(8,128)(2,1)}) %reduce-scatter.28.cloned.1.call-update) | async-done | bytes 49168 | tf_op jit(solution)/shard_map/reduce_scatter | solution.py:284
  657.3 67.3 %reduce-scatter.24.cloned.1.call-done = bf16[64,128]{1,0:T(8,128)(2,1)} async-done(((bf16[1024,128]{1,0:T(8,128)(2,1)}), bf16[64,128]{1,0:T(8,128)(2,1)}) %reduce-scatter.24.cloned.1.call-update) | async-done | bytes 16400 | tf_op jit(solution)/shard_map/reduce_scatter | solution.py:278
  725.9 67.6 %reduce-scatter.22.cloned.1.call-done = bf16[64,128]{1,0:T(8,128)(2,1)} async-done(((bf16[1024,128]{1,0:T(8,128)(2,1)}), bf16[64,128]{1,0:T(8,128)(2,1)}) %reduce-scatter.22.cloned.1.call-update) | async-done | bytes 16400 | tf_op jit(solution)/shard_map/reduce_scatter | solution.py:275
  794.9 67.3 %reduce-scatter.26.cloned.1.call-done = bf16[256,64]{0,1:T(8,128)(2,1)} async-done(((bf16[256,1024]{0,1:T(8,128)(2,1)}), bf16[256,64]{0,1:T(8,128)(2,1)}) %reduce-scatter.26.cloned.1.call-update) | async-done | bytes 32784 | tf_op jit(solution)/shard_map/reduce_scatter | solution.py:281
  863.5 66.9 %reduce-scatter.20.cloned.1.call-done = bf16[64,256]{1,0:T(8,128)(2,1)} async-done(((bf16[1024,256]{1,0:T(8,128)(2,1)}), bf16[64,256]{1,0:T(8,128)(2,1)}) %reduce-scatter.20.cloned.1.call-update) | async-done | bytes 32784 | tf_op jit(solution)/shard_map/reduce_scatter | solution.py:272
  931.8 54.2 %reduce-scatter.18.cloned.1.call-done = bf16[128,1024]{1,0:T(8,128)(2,1)} async-done(((bf16[1024,1024]{1,0:T(8,128)(2,1)}), bf16[128,1024]{1,0:T(8,128)(2,1)}) %reduce-scatter.18.cloned.1.call-update) | async-done | bytes 262160 | tf_op jit(solution)/shard_map/reduce_scatter | solution.py:256
  987.2 66.2 %all-reduce.7 = (f32[1024]{0:T(1024)}, f32[128]{0:T(128)}, f32[128]{0:T(128)}, f32[1024]{0:T(1024)}) all-reduce(f32[1024]{0:T(1024)S(1)} %get-tuple-element.331, f32[128]{0:T(128)S(1)} %get-tuple-element.325, f32[128]{0:T(128)S(1)} %get-tuple-element.327, f32[1024]{0:T(1024)S(1)} %copy-done.47), channel_id=1, replica_groups=mesh['dp'=16,'tensor'=8] {'dp','tensor'}, use_global_device_ids=true, to_apply=%region_22.23 | all-reduce | flops 2304 | bytes 18432 | tf_op jit(solution)/shard_map/psum | solution.py:294
  (292 shorter events, 131.1 us)
Async XLA Ops:
  7.2 57.9 %copy-start.45 = (bf16[64,256]{1,0:T(8,128)(2,1)S(1)}, bf16[64,256]{1,0:T(8,128)(2,1)}, u32[]{:S(2)}) copy-start(bf16[64,256]{1,0:T(8,128)(2,1)} %param.23) | copy-start | bytes 98308
  7.2 81.9 %copy-start.46 = (bf16[256,64]{0,1:T(8,128)(2,1)S(1)}, bf16[256,64]{0,1:T(8,128)(2,1)}, u32[]{:S(2)}) copy-start(bf16[256,64]{0,1:T(8,128)(2,1)} %param.26) | copy-start | bytes 98308
  7.2 105.2 %all-gather.5.cloned.1.call-start = ((), (), s32[]{:S(2)}) async-start(), calls=%async_computation.11 | async-start | bytes 2359296 | tf_op jit(solution)/shard_map/all_gather | solution.py:101
  10.2 199.1 %reduce-scatter.12.cloned.1.call-start = ((), (), s32[]{:S(2)}) async-start(), calls=%async_computation.12 | async-start | bytes 2359296 | tf_op jit(solution)/shard_map/reduce_scatter | solution.py:147
  41.7 73.2 %copy-start.25 = (bf16[1024,128]{1,0:T(8,128)(2,1)}, bf16[1024,128]{1,0:T(8,128)(2,1)S(1)}, u32[]{:S(2)}) copy-start(bf16[1024,128]{1,0:T(8,128)(2,1)S(1)} %all_gather.42) | copy-start | bytes 786436
  64.1 57.9 %copy-start.20 = (bf16[1024,128]{1,0:T(8,128)(2,1)}, bf16[1024,128]{1,0:T(8,128)(2,1)S(1)}, u32[]{:S(2)}) copy-start(bf16[1024,128]{1,0:T(8,128)(2,1)S(1)} %all_gather.41) | copy-start | bytes 786436
  153.9 55.4 %copy-start.3 = (bf16[128,1024]{1,0:T(8,128)(2,1)S(1)}, bf16[128,1024]{1,0:T(8,128)(2,1)}, u32[]{:S(2)}) copy-start(bf16[128,1024]{1,0:T(8,128)(2,1)} %param.18) | copy-start | bytes 786436
  157.1 155.9 %all-gather.7.cloned.1.call-start = ((), (), s32[]{:S(2)}) async-start(), calls=%async_computation.13 | async-start | bytes 2359296 | tf_op jit(solution)/shard_map/all_gather | solution.py:155
  212.2 120.1 %all-gather.9.cloned.1.call-start = ((), (), s32[]{:S(2)}) async-start(), calls=%async_computation.15 | async-start | bytes 2359296 | tf_op jit(solution)/shard_map/all_gather | solution.py:177
  212.8 181.7 %reduce-scatter.16.cloned.1.call-start = ((), (), s32[]{:S(2)}) async-start(), calls=%async_computation.16 | async-start | bytes 2359296 | tf_op jit(solution)/shard_map/reduce_scatter | solution.py:182
  342.2 54.1 %copy-start.62 = (f32[128]{0:T(128)S(1)}, f32[128]{0:T(128)}, u32[]{:S(2)}) copy-start(f32[128]{0:T(128)} %copy-done.61) | copy-start | bytes 1540
  342.2 54.1 %copy-start.22 = (bf16[128,1024]{1,0:T(8,128)(2,1)S(1)}, bf16[128,1024]{1,0:T(8,128)(2,1)}, u32[]{:S(2)}) copy-start(bf16[128,1024]{1,0:T(8,128)(2,1)} %param.31) | copy-start | bytes 786436
  342.2 107.5 %all-gather.11.cloned.1.call-start = ((), (), s32[]{:S(2)}) async-start(), calls=%async_computation.17 | async-start | bytes 2359296 | tf_op jit(solution)/shard_map/all_gather | solution.py:195
  398.2 131.0 %reduce-scatter.32.cloned.1.call-start = ((), (), s32[]{:S(2)}) async-start(), calls=%async_computation.25 | async-start | bytes 835584 | tf_op jit(solution)/shard_map/reduce_scatter | solution.py:290
  402.3 184.5 %reduce-scatter.30.cloned.1.call-start = ((), (), s32[]{:S(2)}) async-start(), calls=%async_computation.24 | async-start | bytes 835584 | tf_op jit(solution)/shard_map/reduce_scatter | solution.py:287
  406.4 249.4 %reduce-scatter.28.cloned.1.call-start = ((), (), s32[]{:S(2)}) async-start(), calls=%async_computation.23 | async-start | bytes 835584 | tf_op jit(solution)/shard_map/reduce_scatter | solution.py:284
  410.3 314.3 %reduce-scatter.24.cloned.1.call-start = ((), (), s32[]{:S(2)}) async-start(), calls=%async_computation.21 | async-start | bytes 278528 | tf_op jit(solution)/shard_map/reduce_scatter | solution.py:278
  500.9 292.7 %reduce-scatter.22.cloned.1.call-start = ((), (), s32[]{:S(2)}) async-start(), calls=%async_computation.20 | async-start | bytes 278528 | tf_op jit(solution)/shard_map/reduce_scatter | solution.py:275
  505.6 356.6 %reduce-scatter.26.cloned.1.call-start = ((), (), s32[]{:S(2)}) async-start(), calls=%async_computation.22 | async-start | bytes 557056 | tf_op jit(solution)/shard_map/reduce_scatter | solution.py:281
  511.5 418.9 %reduce-scatter.20.cloned.1.call-start = ((), (), s32[]{:S(2)}) async-start(), calls=%async_computation.19 | async-start | bytes 557056 | tf_op jit(solution)/shard_map/reduce_scatter | solution.py:272
  519.7 466.3 %reduce-scatter.18.cloned.1.call-start = ((), (), s32[]{:S(2)}) async-start(), calls=%async_computation.18 | async-start | bytes 2359296 | tf_op jit(solution)/shard_map/reduce_scatter | solution.py:256
  525.1 528.3 %reduce-scatter.14.cloned.1.call-start = ((), (), s32[]{:S(2)}) async-start(), calls=%async_computation.14 | async-start | bytes 2359296 | tf_op jit(solution)/shard_map/reduce_scatter | solution.py:160
  529.1 456.9 %copy-start.4 = (bf16[128,1024]{1,0:T(8,128)(2,1)S(1)}, bf16[128,1024]{1,0:T(8,128)(2,1)}, u32[]{:S(2)}) copy-start(bf16[128,1024]{1,0:T(8,128)(2,1)} %param.18) | copy-start | bytes 786436
  529.1 456.9 %copy-start.42 = (f32[1024]{0:T(1024)S(1)}, f32[1024]{0:T(1024)}, u32[]{:S(2)}) copy-start(f32[1024]{0:T(1024)} %param.20) | copy-start | bytes 12292
  529.1 456.9 %copy-start.56 = (f32[128]{0:T(128)S(1)}, f32[128]{0:T(128)}, u32[]{:S(2)}) copy-start(f32[128]{0:T(128)} %copy-done.55) | copy-start | bytes 1540
  529.1 458.1 %copy-start.47 = (f32[1024]{0:T(1024)S(1)}, f32[1024]{0:T(1024)}, u32[]{:S(2)}) copy-start(f32[1024]{0:T(1024)} %get-tuple-element.329) | copy-start | bytes 12292
  529.1 524.3 %copy-start.60 = (f32[128]{0:T(128)S(1)}, f32[128]{0:T(128)}, u32[]{:S(2)}) copy-start(f32[128]{0:T(128)} %copy-done.59) | copy-start | bytes 1540
  529.1 524.3 %copy-start.9 = (bf16[128,1024]{1,0:T(8,128)(2,1)S(1)}, bf16[128,1024]{1,0:T(8,128)(2,1)}, u32[]{:S(2)}) copy-start(bf16[128,1024]{1,0:T(8,128)(2,1)} %reduce-scatter.12.cloned.1.call-done) | copy-start | bytes 786436
  529.1 524.3 %copy-start.23 = (bf16[128,1024]{1,0:T(8,128)(2,1)S(1)}, bf16[128,1024]{1,0:T(8,128)(2,1)}, u32[]{:S(2)}) copy-start(bf16[128,1024]{1,0:T(8,128)(2,1)} %param.31) | copy-start | bytes 786436
  529.1 524.3 %copy-start.24 = (bf16[128,1024]{1,0:T(8,128)(2,1)S(1)}, bf16[128,1024]{1,0:T(8,128)(2,1)}, u32[]{:S(2)}) copy-start(bf16[128,1024]{1,0:T(8,128)(2,1)} %reduce-scatter.16.cloned.1.call-done) | copy-start | bytes 786436
  529.1 524.3 %copy-start.50 = (f32[128]{0:T(128)S(1)}, f32[128]{0:T(128)}, u32[]{:S(2)}) copy-start(f32[128]{0:T(128)} %copy-done.48) | copy-start | bytes 1540
  529.1 524.3 %copy-start.58 = (f32[128]{0:T(128)S(1)}, f32[128]{0:T(128)}, u32[]{:S(2)}) copy-start(f32[128]{0:T(128)} %copy-done.57) | copy-start | bytes 1540
  (49 other events, 374.5 us)
Sparse Core Ops, SparseCore 0:
  10.3 59.5 all-gather.4
  157.2 52.0 reduce-scatter.11
  212.4 63.1 all-gather.6
  277.0 55.3 all-gather.8
  342.4 52.0 reduce-scatter.15
  398.3 51.3 all-gather.10
  453.5 63.8 reduce-scatter.31
  521.7 65.1 reduce-scatter.29
  590.7 65.1 reduce-scatter.27
  660.4 64.1 reduce-scatter.23
  729.3 64.2 reduce-scatter.21
  797.5 64.5 reduce-scatter.25
  865.8 64.5 reduce-scatter.19
  932.8 53.1 reduce-scatter.17
  988.3 52.2 reduce-scatter.13
where the time goes:
time: 1070 us; the launch traced here: 1060 us
  waiting for transfers between devices  604 us (56%)
  blocking collectives  265 us (25%)
  matrix products  85.8 us (8%)
  other arithmetic  55.1 us (5%)
  local copies, waits for them, and re-layouts  29.7 us (3%)
  between operations  15.1 us (1%)
    reduce_scatter x1, waiting for transfers between devices, per_device(): lax.psum_scatter(grad_key_mat.astype(jnp.bfloat16), 'dp', scatter_dimensi...  67.6 us
    reduce_scatter x1, waiting for transfers between devices, per_device(): lax.psum_scatter(grad_gate_mat.astype(jnp.bfloat16), 'dp', scatter_dimens...  67.5 us
    reduce_scatter x1, waiting for transfers between devices, per_device(): lax.psum_scatter(grad_value_mat.astype(jnp.bfloat16), 'dp', scatter_dimen...  67.3 us
    reduce_scatter x1, waiting for transfers between devices, per_device(): lax.psum_scatter(grad_out_mat.astype(jnp.bfloat16), 'dp', scatter_dimensi...  67.3 us
    reduce_scatter x1, waiting for transfers between devices, per_device(): lax.psum_scatter(grad_query_mat.astype(jnp.bfloat16), 'dp', scatter_dimen...  66.9 us
    psum x1, blocking collectives, per_device(): lax.psum((grad_first, grad_query_gain, grad_key_gain, grad_second), ('dp'...  66.2 us
    reduce_scatter x1, waiting for transfers between devices, per_device(): lax.psum_scatter(grad_up_mat.astype(jnp.bfloat16), 'dp', scatter_dimensio...  56.1 us
    dot_general x21, matrix products, dot_float(): return jnp.dot(left_side, right_side, preferred_element_type=jnp.float32)  55.9 us
  transfers between devices with their start and end apart: 15, of which 11 were waited for; matrix products, arithmetic and copies ran while one was open for 10% of the time, Pallas kernels for 0%

commit v1 on v0

v1 whole, which is shorter than its diff:
```python
import jax
import jax.numpy as jnp
import numpy as np
from jax import lax
from jax.sharding import Mesh
from jax.sharding import PartitionSpec as P

EPSILON = 1e-06
ROPE_BASE = 1000000.0
NEG_LARGE = -1e30
BF16 = jnp.bfloat16
F32 = jnp.float32

SIZES = {"z": 4, "h": 2, "c": 2, "y": 4, "l": 2}
DP_RINGS = (("h", "l"), ("z",))


def ring_size(axes):
    return int(np.prod([SIZES[a] for a in axes]))


def fetch(value, axes, step):
    n = ring_size(axes)
    return lax.ppermute(value, axes, [(i, (i - step) % n) for i in range(n)])


def send(value, axes, step):
    n = ring_size(axes)
    return lax.ppermute(value, axes, [(i, (i + step) % n) for i in range(n)])


def core_swap(value):
    return lax.ppermute(value, ("c",), [(0, 1), (1, 0)])


def remap(value):
    pairs = []
    for c in range(2):
        for y in range(4):
            for l in range(2):
                pairs.append(((c * 4 + y) * 2 + l, (l * 4 + y) * 2 + c))
    return lax.ppermute(value, ("c", "y", "l"), pairs)


def dot_nn(a, b):
    return lax.dot_general(a, b, (((1,), (0,)), ((), ())), preferred_element_type=F32)


def dot_nt(a, b):
    return lax.dot_general(a, b, (((1,), (1,)), ((), ())), preferred_element_type=F32)


def dot_tn(a, b):
    return lax.dot_general(a, b, (((0,), (0,)), ((), ())), preferred_element_type=F32)


def gather_tokens(block):
    parts = []
    for s in range(4):
        piece = block if s == 0 else fetch(block, ("y",), s)
        parts += [piece, core_swap(piece)]
    return jnp.concatenate(parts, 0)


def scatter_tokens(partial):
    width = partial.shape[-1]
    blocks = partial.reshape(4, 2, 128, width)
    other = core_swap(blocks[:, 1].astype(BF16))
    mine = blocks[:, 0] + other.astype(F32)
    low = mine.astype(BF16)
    total = mine[0]
    for s in range(1, 4):
        total = total + send(low[s], ("y",), s).astype(F32)
    return total


def rolled(values, axis, amount):
    n = values.shape[axis]
    twice = jnp.concatenate([values, values], axis)
    return lax.dynamic_slice_in_dim(twice, amount, n, axis)


def gather_weights(shard, z, x):
    stage = jnp.stack([shard] + [fetch(shard, ("h", "l"), s) for s in range(1, 4)])
    full = jnp.stack([stage] + [fetch(stage, ("z",), s) for s in range(1, 4)])
    full = rolled(rolled(full, 0, (4 - z) % 4), 1, (4 - x) % 4)
    return full.reshape(1024, shard.shape[1])


def scatter_weights(grad, z, x):
    width = grad.shape[1]
    low = grad.astype(BF16).reshape(4, 4, 64, width)
    low = rolled(rolled(low, 0, z), 1, x)
    total = low[:, 0].astype(F32)
    for s in range(1, 4):
        total = total + send(low[:, s], ("h", "l"), s).astype(F32)
    low = total.astype(BF16)
    result = total[0]
    for s in range(1, 4):
        result = result + send(low[s], ("z",), s).astype(F32)
    return remap(result.astype(BF16)).astype(F32)


def all_sum(values):
    values = values + core_swap(values)
    for axes in (("y",), ("h", "l"), ("z",)):
        got = [send(values, axes, s) for s in range(1, 4)]
        values = (values + got[1]) + (got[0] + got[2])
    return values


def turned(values):
    half = values.shape[-1] // 2
    return jnp.concatenate([-values[..., half:], values[..., :half]], -1)


def norm_forward(values):
    scale = lax.rsqrt(jnp.mean(values * values, -1, keepdims=True) + EPSILON)
    return values * scale, scale


def norm_backward(unit, scale, gain, grad):
    weighted = grad * gain
    return scale * (weighted - unit * jnp.mean(unit * weighted, -1, keepdims=True))


def per_device(
    tokens,
    segment_ids,
    first_gain,
    query_gain,
    key_gain,
    query_weight,
    key_weight,
    value_weight,
    out_weight,
    second_gain,
    gate_weight,
    up_weight,
    down_weight,
    cotangent,
):
    z = lax.axis_index("z")
    x = lax.axis_index("h") * 2 + lax.axis_index("l")
    y = lax.axis_index("y")
    c = lax.axis_index("c")
    tokens = remap(tokens)
    attn_shard = remap(jnp.concatenate([query_weight, key_weight, value_weight], 1))
    seg_row = remap(segment_ids)[0]
    mlp_shard = remap(jnp.concatenate([out_weight.T, gate_weight, up_weight, down_weight.T], 1))
    cotangent = remap(cotangent)

    slot = jnp.arange(8, dtype=jnp.int32)
    block_of = ((y + slot // 2) % 4) * 2 + (slot % 2 + c) % 2
    index = (block_of[:, None] * 128 + jnp.arange(128, dtype=jnp.int32)[None, :]).reshape(1024)
    seg4 = rolled(seg_row.reshape(4, 2, 128), 0, y)
    seg4 = rolled(seg4, 1, c)
    seg = seg4.reshape(1024)
    start = jnp.zeros((1024,), jnp.int32)
    for v in range(1, 4):
        start = start + jnp.where(seg == v, jnp.sum((seg_row < v).astype(jnp.int32)), 0)
    places = (index - start).astype(F32)
    inverse = ROPE_BASE ** (-jnp.arange(0, 128, 2, dtype=F32) / 128)
    phases = places[:, None] * inverse[None, :]
    phases = jnp.concatenate([phases, phases], -1)
    cosine, sine = jnp.cos(phases), jnp.sin(phases)
    allowed = (seg[:, None] == seg[None, :]) & (index[None, :] <= index[:, None])

    input_float = tokens.astype(F32)
    unit_one, scale_one = norm_forward(input_float)
    normed_one = gather_tokens((unit_one * first_gain).astype(BF16))
    attn_full = gather_weights(attn_shard, z, x)
    mlp_full = gather_weights(mlp_shard, z, x)
    cot_all = gather_tokens(cotangent)
    raw = dot_nn(normed_one, attn_full)
    heads = [raw[:, i * 128 : (i + 1) * 128] for i in range(4)]
    gains = [query_gain, query_gain, key_gain]
    units, scales, rots = [], [], []
    for i in range(3):
        unit, scale = norm_forward(heads[i])
        scaled = unit * gains[i]
        units.append(unit)
        scales.append(scale)
        rots.append((scaled * cosine + turned(scaled) * sine).astype(BF16))
    key, value = rots[2], heads[3].astype(BF16)
    score_scale = 128 ** (-0.5)
    outs, logs = [], []
    for i in range(2):
        scores = jnp.where(allowed, dot_nt(rots[i], key) * score_scale, NEG_LARGE)
        top = jnp.max(scores, -1, keepdims=True)
        exponent = jnp.exp(scores - top)
        total = jnp.sum(exponent, -1, keepdims=True)
        prob = (exponent / total).astype(BF16)
        outs.append(dot_nn(prob, value).astype(BF16))
        logs.append(top + jnp.log(total))
    attended = jnp.concatenate(outs, 1)
    out_t = mlp_full[:, :256]
    gate_up = mlp_full[:, 256:1024]
    down_t = mlp_full[:, 1024:]
    hidden = input_float + scatter_tokens(dot_nt(attended, out_t))

    unit_two, scale_two = norm_forward(hidden)
    normed_two = gather_tokens((unit_two * second_gain).astype(BF16))
    gate_up_value = dot_nn(normed_two, gate_up)
    gate, up = gate_up_value[:, :384], gate_up_value[:, 384:]
    sig = jax.nn.sigmoid(gate)
    silu = gate * sig
    act = (silu * up).astype(BF16)
    grad_act = dot_nn(cot_all, down_t)
    grad_gate = (grad_act * up * (sig + silu * (1.0 - sig))).astype(BF16)
    grad_up = (grad_act * silu).astype(BF16)
    grad_gu = jnp.concatenate([grad_gate, grad_up], 1)
    partial_two = dot_nt(grad_gu, gate_up)
    grad_normed_two = scatter_tokens(partial_two)
    layer_out = remap((hidden + scatter_tokens(dot_nt(act, down_t))).astype(BF16))
    second_part = jnp.sum(partial_two * normed_two.astype(F32), 0) / second_gain
    mlp_grad = jnp.concatenate([dot_tn(normed_two, grad_gu), dot_tn(cot_all, act)], 1)
    mlp_owned = scatter_weights(mlp_grad, z, x)

    grad_hidden = cotangent.astype(F32) + norm_backward(
        unit_two, scale_two, second_gain, grad_normed_two
    )
    hidden_grad = gather_tokens(grad_hidden.astype(BF16))
    grad_attended = dot_nn(hidden_grad, out_t).astype(BF16)
    out_owned = scatter_weights(dot_tn(hidden_grad, attended), z, x)
    grad_key = jnp.zeros((1024, 128), F32)
    grad_value = jnp.zeros((1024, 128), F32)
    grad_rot = []
    for i in range(2):
        scores = dot_nt(rots[i], key) * score_scale
        prob = jnp.where(allowed, jnp.exp(scores - logs[i]), 0.0)
        grad_out = grad_attended[:, i * 128 : (i + 1) * 128]
        grad_prob = dot_nt(grad_out, value)
        inner = jnp.sum(prob * grad_prob, -1, keepdims=True)
        grad_scores = (prob * (grad_prob - inner)).astype(BF16)
        grad_rot.append(dot_nn(grad_scores, key) * score_scale)
        grad_key = grad_key + dot_tn(grad_scores, rots[i]) * score_scale
        grad_value = grad_value + dot_tn(prob.astype(BF16), grad_out)
    grad_rot.append(grad_key)
    grad_raw, gain_parts = [], []
    for i in range(3):
        grad = grad_rot[i] * cosine - turned(grad_rot[i]) * sine
        gain_parts.append(jnp.sum(grad * units[i], 0))
        grad_raw.append(norm_backward(units[i], scales[i], gains[i], grad).astype(BF16))
    grad_raw = jnp.concatenate(grad_raw + [grad_value.astype(BF16)], 1)
    partial_one = dot_nt(grad_raw, attn_full)
    grad_normed_one = scatter_tokens(partial_one)
    first_part = jnp.sum(partial_one * normed_one.astype(F32), 0) / first_gain
    attn_owned = scatter_weights(dot_tn(normed_one, grad_raw), z, x)
    sums = all_sum(
        jnp.concatenate([first_part, second_part, gain_parts[0] + gain_parts[1], gain_parts[2]])
    )
    grad_tokens = grad_hidden + norm_backward(unit_one, scale_one, first_gain, grad_normed_one)
    grad_tokens = remap(grad_tokens.astype(BF16))
    return (
        layer_out,
        grad_tokens,
        sums[:1024],
        sums[2048:2176],
        sums[2176:],
        attn_owned[:, :256],
        attn_owned[:, 256:384],
        attn_owned[:, 384:],
        out_owned.T,
        sums[1024:2048],
        mlp_owned[:, :384],
        mlp_owned[:, 384:768],
        mlp_owned[:, 768:].T,
    )


def solution(mesh):
    fine = Mesh(mesh.devices.reshape(4, 2, 2, 4, 2), ("z", "h", "c", "y", "l"))
    dp, tensor = ("z", "h", "c"), ("y", "l")
    rows, cols, trans = P(dp + tensor, None), P(dp, tensor), P(tensor, dp)
    in_specs = (
        rows, P(dp, None), P(), P(), P(), cols, cols, cols, trans, P(), cols, cols, trans, rows,
    )
    out_specs = (rows, rows, P(), P(), P(), cols, cols, cols, trans, P(), cols, cols, trans)
    return jax.shard_map(
        per_device, mesh=fine, in_specs=in_specs, out_specs=out_specs, check_vma=False
    )
```

time: 1070 us -> 361 us (0.34)
  waiting for transfers between devices: 604 us -> 122 us
  blocking collectives: 265 us -> 0 us
  starting transfers between devices: 1.08 us -> 154 us
  matrix products: 85.8 us -> 31.8 us
  other arithmetic: 55.1 us -> 28.2 us
  between operations: 15.1 us -> 2.4 us
  local copies, waits for them, and re-layouts: 29.7 us -> 18.9 us
    reduce_scatter x11 -> x0, waiting for transfers between devices: 551 us -> none  [the longest x1 67.6 us: per_device(): lax.psum_scatter(grad_key_mat.astype(jnp.bfloat16), 'dp', scatter_dimensi...]
    all_gather x7 -> x0, blocking collectives: 199 us -> none  [the longest x1 35.9 us: per_device(): lax.all_gather(gate_weight, 'dp', axis=0, tiled=True)]
    ppermute x0 -> x94, starting transfers between devices: none -> 154 us  [the longest x39 45.4 us: send(): return lax.ppermute(value, axes, [(i, (i + step) % n) for i in range(n)])]
    ppermute x0 -> x94, waiting for transfers between devices: none -> 122 us  [the longest x39 60.7 us: send(): return lax.ppermute(value, axes, [(i, (i + step) % n) for i in range(n)])]
    psum x1 -> x0, blocking collectives: 66.2 us -> none  [per_device(): lax.psum((grad_first, grad_query_gain, grad_key_gain, grad_second), ('dp'...]
    dot_general x35 -> x24, matrix products: 85.8 us -> 31.8 us  [the longest x8 11.8 us: dot_nt(): lax.dot_general(a, b, (((1,), (1,)), ((), ())), preferred_element_type=F32)]
    all_gather x4 -> x0, waiting for transfers between devices: 51.8 us -> none  [the longest x1 39.1 us: per_device(): lax.all_gather(grad_hidden.astype(jnp.bfloat16), 'tensor', axis=0, tiled=...]
    convert_element_type x15 -> x16, other arithmetic: 21.6 us -> 12.9 us  [the longest x4 3.76 us: scatter_tokens(): low = mine.astype(BF16)]
  transfers between devices with their start and end apart: 15 -> 94, of which waited for: 11 -> 39; matrix products, arithmetic and copies ran while one was open for 10% -> 10% of each run, Pallas kernels for 0% -> 0%
where the time goes in v1:
time: 361 us; the launch traced here: 357 us
  starting transfers between devices  154 us (43%)
  waiting for transfers between devices  122 us (34%)
  matrix products  31.8 us (9%)
  other arithmetic  28.2 us (8%)
  local copies, waits for them, and re-layouts  18.9 us (5%)
    ppermute x39, waiting for transfers between devices, send(): return lax.ppermute(value, axes, [(i, (i + step) % n) for i in range(n)])  60.7 us
    ppermute x24, waiting for transfers between devices, fetch(): return lax.ppermute(value, axes, [(i, (i - step) % n) for i in range(n)])  50.3 us
    ppermute x39, starting transfers between devices, send(): return lax.ppermute(value, axes, [(i, (i + step) % n) for i in range(n)])  45.4 us
    ppermute x21, starting transfers between devices, core_swap(): return lax.ppermute(value, ('c',), [(0, 1), (1, 0)])  40.2 us
    ppermute x10, starting transfers between devices, remap(): return lax.ppermute(value, ('c', 'y', 'l'), pairs)  37.7 us
    ppermute x24, starting transfers between devices, fetch(): return lax.ppermute(value, axes, [(i, (i - step) % n) for i in range(n)])  30.2 us
    unnamed x81, local copies, waits for them, and re-layouts  12.6 us
    dot_general x8, matrix products, dot_nt(): lax.dot_general(a, b, (((1,), (1,)), ((), ())), preferred_element_type=F32)  11.8 us
  transfers between devices with their start and end apart: 94, of which 39 were waited for; matrix products, arithmetic and copies ran while one was open for 10% of the time, Pallas kernels for 0%

profile of v1, /device:TPU:1, one launch (start us, length us, event | category | flops | bytes accessed | tf_op | source)
XLA Modules:
  0.0 357.0 jit_solution(15363922874779663461)
XLA Ops:
  1.5 4.5 %collective-permute-start.9 = (bf16[64,512]{1,0:T(8,128)(2,1)S(1)}, bf16[64,512]{1,0:T(8,128)(2,1)S(1)}, u32[]{:S(2)}, u32[]{:S(2)}) collective-permute-start(bf16[64,512]{1,0:T(8,128)(2,1)S(1)} %pad_maximum_fusion.13), channel_id=1, source_target_pairs={{0,0},{1,8},{2,2},{3,10},{4,4},{5,12},{6,6},{7,14},{8,1},{9,9},{10... | collective-permute-start | bytes 196616 | tf_op jit(solution)/shard_map/ppermute | solution.py:42
  7.9 3.6 %collective-permute-start.1 = (s32[1,1024]{1,0:T(1,128)}, s32[1,1024]{1,0:T(1,128)S(1)}, u32[]{:S(2)}, u32[]{:S(2)}) collective-permute-start(s32[1,1024]{1,0:T(1,128)} %param.15), channel_id=1, source_target_pairs={{0,0},{1,8},{2,2},{3,10},{4,4},{5,12},{6,6},{7,14},{8,1},{9,9},{10... | collective-permute-start | bytes 12296 | tf_op jit(solution)/shard_map/ppermute | solution.py:42
  24.4 3.8 %collective-permute-start.13 = (bf16[4,64,512]{2,1,0:T(8,128)(2,1)S(1)}, bf16[4,64,512]{2,1,0:T(8,128)(2,1)S(1)}, u32[]{:S(2)}, u32[]{:S(2)}) collective-permute-start(bf16[4,64,512]{2,1,0:T(8,128)(2,1)S(1)} %pad_maximum_fusion.9), channel_id=1, source_target_pairs={{0,96},{32,0},{64,32},{96,64},{1,97},{33,1},{65,33},{97,65},{2,98}... | collective-permute-start | bytes 786440 | tf_op jit(solution)/shard_map/ppermute | solution.py:24
  35.1 4.6 %collective-permute-start.2 = (bf16[128,1024]{1,0:T(8,128)(2,1)S(1)}, bf16[128,1024]{1,0:T(8,128)(2,1)S(1)}, u32[]{:S(2)}, u32[]{:S(2)}) collective-permute-start(bf16[128,1024]{1,0:T(8,128)(2,1)S(1)} %get-tuple-element.58), channel_id=1, source_target_pairs={{0,8},{8,0},{1,9},{9,1},{2,10},{10,2},{3,11},{11,3},{4,12},{12,4},... | collective-permute-start | bytes 786440 | tf_op jit(solution)/shard_map/ppermute | solution.py:33
  47.8 6.7 %collective-permute-start.4 = (bf16[128,1024]{1,0:T(8,128)(2,1)S(1)}, bf16[128,1024]{1,0:T(8,128)(2,1)S(1)}, u32[]{:S(2)}, u32[]{:S(2)}) collective-permute-start(bf16[128,1024]{1,0:T(8,128)(2,1)S(1)} %collective-permute-done.3), channel_id=1, source_target_pairs={{0,8},{8,0},{1,9},{9,1},{2,10},{10,2},{3,11},{11,3},{4,12},{12,4},... | collective-permute-start | bytes 786440 | tf_op jit(solution)/shard_map/ppermute | solution.py:33
  55.0 3.0 collective-permute-start.21
  74.5 15.6 %collective-permute-done.22 = bf16[4,64,1408]{2,1,0:T(8,128)(2,1)S(1)} collective-permute-done((bf16[4,64,1408]{2,1,0:T(8,128)(2,1)S(1)}, bf16[4,64,1408]{2,1,0:T(8,128)(2,1)S(1)}, u32[]{:S(2)}, u32[]{:S(2)}) %collective-permute-start.22) | collective-permute-done | bytes 720928 | tf_op jit(solution)/shard_map/ppermute | solution.py:24
  99.8 5.2 %collective-permute-done.39 = bf16[128,1024]{1,0:T(8,128)(2,1)S(1)} collective-permute-done((bf16[128,1024]{1,0:T(8,128)(2,1)S(1)}, bf16[128,1024]{1,0:T(8,128)(2,1)S(1)}, u32[]{:S(2)}, u32[]{:S(2)}) %collective-permute-start.39) | collective-permute-done | bytes 262176 | tf_op jit(solution)/shard_map/ppermute | solution.py:42
  104.9 3.8 %collective-permute-start.41 = (bf16[128,1024]{1,0:T(8,128)(2,1)S(1)}, bf16[128,1024]{1,0:T(8,128)(2,1)}, u32[]{:S(2)}, u32[]{:S(2)}) collective-permute-start(bf16[128,1024]{1,0:T(8,128)(2,1)S(1)} %collective-permute-done.39), channel_id=1, source_target_pairs={{0,6},{2,0},{4,2},{6,4},{1,7},{3,1},{5,3},{7,5},{8,14},{10,8},{12,... | collective-permute-start | bytes 786440 | tf_op jit(solution)/shard_map/ppermute | solution.py:24
  109.3 5.5 %collective-permute-done.41 = bf16[128,1024]{1,0:T(8,128)(2,1)} collective-permute-done((bf16[128,1024]{1,0:T(8,128)(2,1)S(1)}, bf16[128,1024]{1,0:T(8,128)(2,1)}, u32[]{:S(2)}, u32[]{:S(2)}) %collective-permute-start.41) | collective-permute-done | bytes 262176 | tf_op jit(solution)/shard_map/ppermute | solution.py:24
  125.3 6.7 %collective-permute-done.24 = bf16[128,1024]{1,0:T(8,128)(2,1)S(1)} collective-permute-done((bf16[128,1024]{1,0:T(8,128)(2,1)S(1)}, bf16[128,1024]{1,0:T(8,128)(2,1)S(1)}, u32[]{:S(2)}, u32[]{:S(2)}) %collective-permute-start.24) | collective-permute-done | bytes 262176 | tf_op jit(solution)/shard_map/ppermute | solution.py:29
  132.0 3.9 %collective-permute-done.25 = bf16[128,1024]{1,0:T(8,128)(2,1)S(1)} collective-permute-done((bf16[128,1024]{1,0:T(8,128)(2,1)S(1)}, bf16[128,1024]{1,0:T(8,128)(2,1)S(1)}, u32[]{:S(2)}, u32[]{:S(2)}) %collective-permute-start.25) | collective-permute-done | bytes 262176 | tf_op jit(solution)/shard_map/ppermute | solution.py:29
  137.5 2.9 collective-permute-start.28
  144.0 2.8 collective-permute-done.28
  146.8 5.8 %collective-permute-start.29 = (bf16[128,1024]{1,0:T(8,128)(2,1)S(1)}, bf16[128,1024]{1,0:T(8,128)(2,1)S(1)}, u32[]{:S(2)}, u32[]{:S(2)}) collective-permute-start(bf16[128,1024]{1,0:T(8,128)(2,1)S(1)} %collective-permute-done.28), channel_id=1, source_target_pairs={{0,8},{8,0},{1,9},{9,1},{2,10},{10,2},{3,11},{11,3},{4,12},{12,4},... | collective-permute-start | bytes 786440 | tf_op jit(solution)/shard_map/ppermute | solution.py:33
  153.4 4.6 %collective-permute-done.32 = bf16[128,1024]{1,0:T(8,128)(2,1)S(1)} collective-permute-done((bf16[128,1024]{1,0:T(8,128)(2,1)S(1)}, bf16[128,1024]{1,0:T(8,128)(2,1)S(1)}, u32[]{:S(2)}, u32[]{:S(2)}) %collective-permute-start.32) | collective-permute-done | bytes 262176 | tf_op jit(solution)/shard_map/ppermute | solution.py:24
  158.0 8.4 %collective-permute-start.33 = (bf16[128,1024]{1,0:T(8,128)(2,1)S(1)}, bf16[128,1024]{1,0:T(8,128)(2,1)S(1)}, u32[]{:S(2)}, u32[]{:S(2)}) collective-permute-start(bf16[128,1024]{1,0:T(8,128)(2,1)S(1)} %collective-permute-done.32), channel_id=1, source_target_pairs={{0,8},{8,0},{1,9},{9,1},{2,10},{10,2},{3,11},{11,3},{4,12},{12,4},... | collective-permute-start | bytes 786440 | tf_op jit(solution)/shard_map/ppermute | solution.py:33
  186.4 8.3 %collective-permute-done.87 = bf16[4,64,1152]{2,1,0:T(8,128)(2,1)S(1)} collective-permute-done((bf16[4,64,1152]{2,1,0:T(8,128)(2,1)S(1)}, bf16[4,64,1152]{2,1,0:T(8,128)(2,1)S(1)}, u32[]{:S(2)}, u32[]{:S(2)}) %collective-permute-start.87) | collective-permute-done | bytes 589856 | tf_op jit(solution)/shard_map/ppermute | solution.py:29
  194.7 13.5 %collective-permute-done.88 = bf16[4,64,1152]{2,1,0:T(8,128)(2,1)S(1)} collective-permute-done((bf16[4,64,1152]{2,1,0:T(8,128)(2,1)S(1)}, bf16[4,64,1152]{2,1,0:T(8,128)(2,1)S(1)}, u32[]{:S(2)}, u32[]{:S(2)}) %collective-permute-start.88) | collective-permute-done | bytes 589856 | tf_op jit(solution)/shard_map/ppermute | solution.py:29
  218.9 2.9 collective-permute-done.35
  224.7 9.0 %collective-permute-start.93 = (bf16[64,1152]{1,0:T(8,128)(2,1)S(1)}, bf16[64,1152]{1,0:T(8,128)(2,1)S(1)}, u32[]{:S(2)}, u32[]{:S(2)}) collective-permute-start(bf16[64,1152]{1,0:T(8,128)(2,1)S(1)} %fusion.107), channel_id=1, source_target_pairs={{0,0},{1,8},{2,2},{3,10},{4,4},{5,12},{6,6},{7,14},{8,1},{9,9},{10... | collective-permute-start | bytes 442376 | tf_op jit(solution)/shard_map/ppermute | solution.py:42
  239.2 3.5 collective-permute-start.52
  245.2 3.8 %collective-permute-start.38 = (bf16[128,1024]{1,0:T(8,128)(2,1)S(1)}, bf16[128,1024]{1,0:T(8,128)(2,1)S(1)}, u32[]{:S(2)}, u32[]{:S(2)}) collective-permute-start(bf16[128,1024]{1,0:T(8,128)(2,1)S(1)} %get-tuple-element.99), channel_id=1, source_target_pairs={{0,0},{1,8},{2,2},{3,10},{4,4},{5,12},{6,6},{7,14},{8,1},{9,9},{10... | collective-permute-start | bytes 786440 | tf_op jit(solution)/shard_map/ppermute | solution.py:42
  249.1 3.6 %collective-permute-done.52 = bf16[128,1024]{1,0:T(8,128)(2,1)S(1)} collective-permute-done((bf16[128,1024]{1,0:T(8,128)(2,1)S(1)}, bf16[128,1024]{1,0:T(8,128)(2,1)S(1)}, u32[]{:S(2)}, u32[]{:S(2)}) %collective-permute-start.52) | collective-permute-done | bytes 262176 | tf_op jit(solution)/shard_map/ppermute | solution.py:24
  255.5 4.0 %collective-permute-done.56 = bf16[128,1024]{1,0:T(8,128)(2,1)S(1)} collective-permute-done((bf16[128,1024]{1,0:T(8,128)(2,1)S(1)}, bf16[128,1024]{1,0:T(8,128)(2,1)S(1)}, u32[]{:S(2)}, u32[]{:S(2)}) %collective-permute-start.56) | collective-permute-done | bytes 262176 | tf_op jit(solution)/shard_map/ppermute | solution.py:24
  268.1 3.4 multiply_convert_fusion.1
  306.1 4.7 %collective-permute-start.58 = (bf16[4,128,1024]{2,1,0:T(8,128)(2,1)S(1)}, bf16[4,128,1024]{2,1,0:T(8,128)(2,1)S(1)}, u32[]{:S(2)}, u32[]{:S(2)}) collective-permute-start(bf16[4,128,1024]{2,1,0:T(8,128)(2,1)S(1)} %fusion.40), channel_id=1, source_target_pairs={{0,8},{8,0},{1,9},{9,1},{2,10},{10,2},{3,11},{11,3},{4,12},{12,4},... | collective-permute-start | bytes 3145736 | tf_op jit(solution)/shard_map/ppermute | solution.py:33
  317.5 4.4 %collective-permute-done.74 = bf16[4,64,512]{2,1,0:T(8,128)(2,1)S(1)} collective-permute-done((bf16[4,64,512]{2,1,0:T(8,128)(2,1)S(1)}, bf16[4,64,512]{2,1,0:T(8,128)(2,1)S(1)}, u32[]{:S(2)}, u32[]{:S(2)}) %collective-permute-start.74) | collective-permute-done | bytes 262176 | tf_op jit(solution)/shard_map/ppermute | solution.py:29
  322.2 5.3 %collective-permute-done.75 = bf16[4,64,512]{2,1,0:T(8,128)(2,1)S(1)} collective-permute-done((bf16[4,64,512]{2,1,0:T(8,128)(2,1)S(1)}, bf16[4,64,512]{2,1,0:T(8,128)(2,1)S(1)}, u32[]{:S(2)}, u32[]{:S(2)}) %collective-permute-start.75) | collective-permute-done | bytes 262176 | tf_op jit(solution)/shard_map/ppermute | solution.py:29
  335.9 4.3 %collective-permute-start.86 = (bf16[64,256]{1,0:T(8,128)(2,1)S(1)}, bf16[64,256]{1,0:T(8,128)(2,1)S(1)}, u32[]{:S(2)}, u32[]{:S(2)}) collective-permute-start(bf16[64,256]{1,0:T(8,128)(2,1)S(1)} %fusion.124), channel_id=1, source_target_pairs={{0,0},{1,8},{2,2},{3,10},{4,4},{5,12},{6,6},{7,14},{8,1},{9,9},{10... | collective-permute-start | bytes 98312 | tf_op jit(solution)/shard_map/ppermute | solution.py:42
  342.2 3.9 %collective-permute-done.60 = bf16[128,1024]{1,0:T(8,128)(2,1)S(1)} collective-permute-done((bf16[128,1024]{1,0:T(8,128)(2,1)S(1)}, bf16[128,1024]{1,0:T(8,128)(2,1)S(1)}, u32[]{:S(2)}, u32[]{:S(2)}) %collective-permute-start.60) | collective-permute-done | bytes 262176 | tf_op jit(solution)/shard_map/ppermute | solution.py:29
  347.2 4.1 %collective-permute-start.62 = (bf16[128,1024]{1,0:T(8,128)(2,1)S(1)}, bf16[128,1024]{1,0:T(8,128)(2,1)S(1)}, u32[]{:S(2)}, u32[]{:S(2)}) collective-permute-start(bf16[128,1024]{1,0:T(8,128)(2,1)S(1)} %fusion.53), channel_id=1, source_target_pairs={{0,0},{1,8},{2,2},{3,10},{4,4},{5,12},{6,6},{7,14},{8,1},{9,9},{10... | collective-permute-start | bytes 786440 | tf_op jit(solution)/shard_map/ppermute | solution.py:42
  (365 shorter events, 184.1 us)
Async XLA Ops:
  1.5 15.8 %collective-permute-start.9 = (bf16[64,512]{1,0:T(8,128)(2,1)S(1)}, bf16[64,512]{1,0:T(8,128)(2,1)S(1)}, u32[]{:S(2)}, u32[]{:S(2)}) collective-permute-start(bf16[64,512]{1,0:T(8,128)(2,1)S(1)} %pad_maximum_fusion.13), channel_id=1, source_target_pairs={{0,0},{1,8},{2,2},{3,10},{4,4},{5,12},{6,6},{7,14},{8,1},{9,9},{10... | collective-permute-start | bytes 196616 | tf_op jit(solution)/shard_map/ppermute | solution.py:42
  6.0 24.2 %collective-permute-start = (bf16[128,1024]{1,0:T(8,128)(2,1)}, bf16[128,1024]{1,0:T(8,128)(2,1)S(1)}, u32[]{:S(2)}, u32[]{:S(2)}) collective-permute-start(bf16[128,1024]{1,0:T(8,128)(2,1)} %param.14), channel_id=1, source_target_pairs={{0,0},{1,8},{2,2},{3,10},{4,4},{5,12},{6,6},{7,14},{8,1},{9,9},{10... | collective-permute-start | bytes 786440 | tf_op jit(solution)/shard_map/ppermute | solution.py:42
  12.4 15.8 %collective-permute-start.16 = (bf16[64,1408]{1,0:T(8,128)(2,1)S(1)}, bf16[64,1408]{1,0:T(8,128)(2,1)S(1)}, u32[]{:S(2)}, u32[]{:S(2)}) collective-permute-start(bf16[64,1408]{1,0:T(8,128)(2,1)S(1)} %pad_maximum_fusion.10), channel_id=1, source_target_pairs={{0,0},{1,8},{2,2},{3,10},{4,4},{5,12},{6,6},{7,14},{8,1},{9,9},{10... | collective-permute-start | bytes 540680 | tf_op jit(solution)/shard_map/ppermute | solution.py:42
  24.4 18.2 %collective-permute-start.13 = (bf16[4,64,512]{2,1,0:T(8,128)(2,1)S(1)}, bf16[4,64,512]{2,1,0:T(8,128)(2,1)S(1)}, u32[]{:S(2)}, u32[]{:S(2)}) collective-permute-start(bf16[4,64,512]{2,1,0:T(8,128)(2,1)S(1)} %pad_maximum_fusion.9), channel_id=1, source_target_pairs={{0,96},{32,0},{64,32},{96,64},{1,97},{33,1},{65,33},{97,65},{2,98}... | collective-permute-start | bytes 786440 | tf_op jit(solution)/shard_map/ppermute | solution.py:24
  28.2 14.9 %collective-permute-start.14 = (bf16[4,64,512]{2,1,0:T(8,128)(2,1)S(1)}, bf16[4,64,512]{2,1,0:T(8,128)(2,1)S(1)}, u32[]{:S(2)}, u32[]{:S(2)}) collective-permute-start(bf16[4,64,512]{2,1,0:T(8,128)(2,1)S(1)} %pad_maximum_fusion.9), channel_id=1, source_target_pairs={{0,64},{32,96},{64,0},{96,32},{1,65},{33,97},{65,1},{97,33},{2,66}... | collective-permute-start | bytes 786440 | tf_op jit(solution)/shard_map/ppermute | solution.py:24
  35.1 19.8 %collective-permute-start.2 = (bf16[128,1024]{1,0:T(8,128)(2,1)S(1)}, bf16[128,1024]{1,0:T(8,128)(2,1)S(1)}, u32[]{:S(2)}, u32[]{:S(2)}) collective-permute-start(bf16[128,1024]{1,0:T(8,128)(2,1)S(1)} %get-tuple-element.58), channel_id=1, source_target_pairs={{0,8},{8,0},{1,9},{9,1},{2,10},{10,2},{3,11},{11,3},{4,12},{12,4},... | collective-permute-start | bytes 786440 | tf_op jit(solution)/shard_map/ppermute | solution.py:33
  42.6 15.4 %collective-permute-start.5 = (bf16[128,1024]{1,0:T(8,128)(2,1)S(1)}, bf16[128,1024]{1,0:T(8,128)(2,1)S(1)}, u32[]{:S(2)}, u32[]{:S(2)}) collective-permute-start(bf16[128,1024]{1,0:T(8,128)(2,1)S(1)} %get-tuple-element.58), channel_id=1, source_target_pairs={{0,4},{2,6},{4,0},{6,2},{1,5},{3,7},{5,1},{7,3},{8,12},{10,14},{12... | collective-permute-start | bytes 786440 | tf_op jit(solution)/shard_map/ppermute | solution.py:24
  43.1 15.3 %collective-permute-start.7 = (bf16[128,1024]{1,0:T(8,128)(2,1)S(1)}, bf16[128,1024]{1,0:T(8,128)(2,1)S(1)}, u32[]{:S(2)}, u32[]{:S(2)}) collective-permute-start(bf16[128,1024]{1,0:T(8,128)(2,1)S(1)} %get-tuple-element.58), channel_id=1, source_target_pairs={{0,2},{2,4},{4,6},{6,0},{1,3},{3,5},{5,7},{7,1},{8,10},{10,12},{12... | collective-permute-start | bytes 786440 | tf_op jit(solution)/shard_map/ppermute | solution.py:24
  43.9 29.4 %collective-permute-start.20 = (bf16[4,64,1408]{2,1,0:T(8,128)(2,1)S(1)}, bf16[4,64,1408]{2,1,0:T(8,128)(2,1)S(1)}, u32[]{:S(2)}, u32[]{:S(2)}) collective-permute-start(bf16[4,64,1408]{2,1,0:T(8,128)(2,1)S(1)} %pad_maximum_fusion.4), channel_id=1, source_target_pairs={{0,96},{32,0},{64,32},{96,64},{1,97},{33,1},{65,33},{97,65},{2,98}... | collective-permute-start | bytes 2162696 | tf_op jit(solution)/shard_map/ppermute | solution.py:24
  55.0 19.4 %collective-permute-start.21 = (bf16[4,64,1408]{2,1,0:T(8,128)(2,1)S(1)}, bf16[4,64,1408]{2,1,0:T(8,128)(2,1)S(1)}, u32[]{:S(2)}, u32[]{:S(2)}) collective-permute-start(bf16[4,64,1408]{2,1,0:T(8,128)(2,1)S(1)} %pad_maximum_fusion.4), channel_id=1, source_target_pairs={{0,64},{32,96},{64,0},{96,32},{1,65},{33,97},{65,1},{97,33},{2,66}... | collective-permute-start | bytes 2162696 | tf_op jit(solution)/shard_map/ppermute | solution.py:24
  58.4 31.7 %collective-permute-start.22 = (bf16[4,64,1408]{2,1,0:T(8,128)(2,1)S(1)}, bf16[4,64,1408]{2,1,0:T(8,128)(2,1)S(1)}, u32[]{:S(2)}, u32[]{:S(2)}) collective-permute-start(bf16[4,64,1408]{2,1,0:T(8,128)(2,1)S(1)} %pad_maximum_fusion.4), channel_id=1, source_target_pairs={{0,32},{32,64},{64,96},{96,0},{1,33},{33,65},{65,97},{97,1},{2,34}... | collective-permute-start | bytes 2162696 | tf_op jit(solution)/shard_map/ppermute | solution.py:24
  96.8 23.3 %collective-permute-start.23 = (bf16[4,128,1024]{2,1,0:T(8,128)(2,1)}, bf16[4,128,1024]{2,1,0:T(8,128)(2,1)}, u32[]{:S(2)}, u32[]{:S(2)}) collective-permute-start(bf16[4,128,1024]{2,1,0:T(8,128)(2,1)} %fusion.37), channel_id=1, source_target_pairs={{0,8},{8,0},{1,9},{9,1},{2,10},{10,2},{3,11},{11,3},{4,12},{12,4},... | collective-permute-start | bytes 3145736 | tf_op jit(solution)/shard_map/ppermute | solution.py:33
  115.7 27.0 %collective-permute-start.44 = (bf16[128,1024]{1,0:T(8,128)(2,1)}, bf16[128,1024]{1,0:T(8,128)(2,1)S(1)}, u32[]{:S(2)}, u32[]{:S(2)}) collective-permute-start(bf16[128,1024]{1,0:T(8,128)(2,1)} %collective-permute-done.43), channel_id=1, source_target_pairs={{0,8},{8,0},{1,9},{9,1},{2,10},{10,2},{3,11},{11,3},{4,12},{12,4},... | collective-permute-start | bytes 786440 | tf_op jit(solution)/shard_map/ppermute | solution.py:33
  118.1 34.5 %collective-permute-start.46 = (bf16[128,1024]{1,0:T(8,128)(2,1)}, bf16[128,1024]{1,0:T(8,128)(2,1)S(1)}, u32[]{:S(2)}, u32[]{:S(2)}) collective-permute-start(bf16[128,1024]{1,0:T(8,128)(2,1)} %collective-permute-done.45), channel_id=1, source_target_pairs={{0,8},{8,0},{1,9},{9,1},{2,10},{10,2},{3,11},{11,3},{4,12},{12,4},... | collective-permute-start | bytes 786440 | tf_op jit(solution)/shard_map/ppermute | solution.py:33
  146.8 19.7 %collective-permute-start.29 = (bf16[128,1024]{1,0:T(8,128)(2,1)S(1)}, bf16[128,1024]{1,0:T(8,128)(2,1)S(1)}, u32[]{:S(2)}, u32[]{:S(2)}) collective-permute-start(bf16[128,1024]{1,0:T(8,128)(2,1)S(1)} %collective-permute-done.28), channel_id=1, source_target_pairs={{0,8},{8,0},{1,9},{9,1},{2,10},{10,2},{3,11},{11,3},{4,12},{12,4},... | collective-permute-start | bytes 786440 | tf_op jit(solution)/shard_map/ppermute | solution.py:33
  178.4 16.4 %collective-permute-start.87 = (bf16[4,64,1152]{2,1,0:T(8,128)(2,1)S(1)}, bf16[4,64,1152]{2,1,0:T(8,128)(2,1)S(1)}, u32[]{:S(2)}, u32[]{:S(2)}) collective-permute-start(bf16[4,64,1152]{2,1,0:T(8,128)(2,1)S(1)} %get-tuple-element.62), channel_id=1, source_target_pairs={{0,1},{1,16},{16,17},{17,0},{2,3},{3,18},{18,19},{19,2},{4,5},{5,2... | collective-permute-start | bytes 1769480 | tf_op jit(solution)/shard_map/ppermute | solution.py:29
  180.2 28.1 %collective-permute-start.88 = (bf16[4,64,1152]{2,1,0:T(8,128)(2,1)S(1)}, bf16[4,64,1152]{2,1,0:T(8,128)(2,1)S(1)}, u32[]{:S(2)}, u32[]{:S(2)}) collective-permute-start(bf16[4,64,1152]{2,1,0:T(8,128)(2,1)S(1)} %get-tuple-element.64), channel_id=1, source_target_pairs={{0,16},{1,17},{16,0},{17,1},{2,18},{3,19},{18,2},{19,3},{4,20},{5,... | collective-permute-start | bytes 1769480 | tf_op jit(solution)/shard_map/ppermute | solution.py:29
  182.5 25.7 %collective-permute-start.89 = (bf16[4,64,1152]{2,1,0:T(8,128)(2,1)S(1)}, bf16[4,64,1152]{2,1,0:T(8,128)(2,1)S(1)}, u32[]{:S(2)}, u32[]{:S(2)}) collective-permute-start(bf16[4,64,1152]{2,1,0:T(8,128)(2,1)S(1)} %get-tuple-element.63), channel_id=1, source_target_pairs={{0,17},{1,0},{16,1},{17,16},{2,19},{3,2},{18,3},{19,18},{4,21},{5,... | collective-permute-start | bytes 1769480 | tf_op jit(solution)/shard_map/ppermute | solution.py:29
  182.8 29.8 %collective-permute-start.34 = (bf16[4,128,1024]{2,1,0:T(8,128)(2,1)S(1)}, bf16[4,128,1024]{2,1,0:T(8,128)(2,1)S(1)}, u32[]{:S(2)}, u32[]{:S(2)}) collective-permute-start(bf16[4,128,1024]{2,1,0:T(8,128)(2,1)S(1)} %fusion.38), channel_id=1, source_target_pairs={{0,8},{8,0},{1,9},{9,1},{2,10},{10,2},{3,11},{11,3},{4,12},{12,4},... | collective-permute-start | bytes 3145736 | tf_op jit(solution)/shard_map/ppermute | solution.py:33
  186.3 26.9 %collective-permute-start.47 = (bf16[4,128,1024]{2,1,0:T(8,128)(2,1)S(1)}, bf16[4,128,1024]{2,1,0:T(8,128)(2,1)S(1)}, u32[]{:S(2)}, u32[]{:S(2)}) collective-permute-start(bf16[4,128,1024]{2,1,0:T(8,128)(2,1)S(1)} %fusion.39), channel_id=1, source_target_pairs={{0,8},{8,0},{1,9},{9,1},{2,10},{10,2},{3,11},{11,3},{4,12},{12,4},... | collective-permute-start | bytes 3145736 | tf_op jit(solution)/shard_map/ppermute | solution.py:33
  215.2 18.5 %collective-permute-start.37 = (bf16[128,1024]{1,0:T(8,128)(2,1)S(1)}, bf16[128,1024]{1,0:T(8,128)(2,1)S(1)}, u32[]{:S(2)}, u32[]{:S(2)}) collective-permute-start(bf16[128,1024]{1,0:T(8,128)(2,1)S(1)} %get-tuple-element.81), channel_id=1, source_target_pairs={{0,6},{2,0},{4,2},{6,4},{1,7},{3,1},{5,3},{7,5},{8,14},{10,8},{12,... | collective-permute-start | bytes 786440 | tf_op jit(solution)/shard_map/ppermute | solution.py:29
  216.7 17.0 %collective-permute-start.48 = (bf16[128,1024]{1,0:T(8,128)(2,1)S(1)}, bf16[128,1024]{1,0:T(8,128)(2,1)S(1)}, u32[]{:S(2)}, u32[]{:S(2)}) collective-permute-start(bf16[128,1024]{1,0:T(8,128)(2,1)S(1)} %get-tuple-element.77), channel_id=1, source_target_pairs={{0,2},{2,4},{4,6},{6,0},{1,3},{3,5},{5,7},{7,1},{8,10},{10,12},{12... | collective-permute-start | bytes 786440 | tf_op jit(solution)/shard_map/ppermute | solution.py:29
  217.5 18.4 %collective-permute-start.49 = (bf16[128,1024]{1,0:T(8,128)(2,1)S(1)}, bf16[128,1024]{1,0:T(8,128)(2,1)S(1)}, u32[]{:S(2)}, u32[]{:S(2)}) collective-permute-start(bf16[128,1024]{1,0:T(8,128)(2,1)S(1)} %get-tuple-element.79), channel_id=1, source_target_pairs={{0,4},{2,6},{4,0},{6,2},{1,5},{3,7},{5,1},{7,3},{8,12},{10,14},{12... | collective-permute-start | bytes 786440 | tf_op jit(solution)/shard_map/ppermute | solution.py:29
  221.9 16.6 %collective-permute-start.50 = (bf16[128,1024]{1,0:T(8,128)(2,1)S(1)}, bf16[128,1024]{1,0:T(8,128)(2,1)S(1)}, u32[]{:S(2)}, u32[]{:S(2)}) collective-permute-start(bf16[128,1024]{1,0:T(8,128)(2,1)S(1)} %get-tuple-element.78), channel_id=1, source_target_pairs={{0,6},{2,0},{4,2},{6,4},{1,7},{3,1},{5,3},{7,5},{8,14},{10,8},{12,... | collective-permute-start | bytes 786440 | tf_op jit(solution)/shard_map/ppermute | solution.py:29
  224.7 19.4 %collective-permute-start.93 = (bf16[64,1152]{1,0:T(8,128)(2,1)S(1)}, bf16[64,1152]{1,0:T(8,128)(2,1)S(1)}, u32[]{:S(2)}, u32[]{:S(2)}) collective-permute-start(bf16[64,1152]{1,0:T(8,128)(2,1)S(1)} %fusion.107), channel_id=1, source_target_pairs={{0,0},{1,8},{2,2},{3,10},{4,4},{5,12},{6,6},{7,14},{8,1},{9,9},{10... | collective-permute-start | bytes 442376 | tf_op jit(solution)/shard_map/ppermute | solution.py:42
  245.2 14.7 %collective-permute-start.38 = (bf16[128,1024]{1,0:T(8,128)(2,1)S(1)}, bf16[128,1024]{1,0:T(8,128)(2,1)S(1)}, u32[]{:S(2)}, u32[]{:S(2)}) collective-permute-start(bf16[128,1024]{1,0:T(8,128)(2,1)S(1)} %get-tuple-element.99), channel_id=1, source_target_pairs={{0,0},{1,8},{2,2},{3,10},{4,4},{5,12},{6,6},{7,14},{8,1},{9,9},{10... | collective-permute-start | bytes 786440 | tf_op jit(solution)/shard_map/ppermute | solution.py:42
  285.0 26.9 %collective-permute-start.80 = (bf16[4,64,256]{2,1,0:T(8,128)(2,1)S(1)}, bf16[4,64,256]{2,1,0:T(8,128)(2,1)S(1)}, u32[]{:S(2)}, u32[]{:S(2)}) collective-permute-start(bf16[4,64,256]{2,1,0:T(8,128)(2,1)S(1)} %get-tuple-element.89), channel_id=1, source_target_pairs={{0,1},{1,16},{16,17},{17,0},{2,3},{3,18},{18,19},{19,2},{4,5},{5,2... | collective-permute-start | bytes 393224 | tf_op jit(solution)/shard_map/ppermute | solution.py:29
  286.5 27.6 %collective-permute-start.81 = (bf16[4,64,256]{2,1,0:T(8,128)(2,1)S(1)}, bf16[4,64,256]{2,1,0:T(8,128)(2,1)S(1)}, u32[]{:S(2)}, u32[]{:S(2)}) collective-permute-start(bf16[4,64,256]{2,1,0:T(8,128)(2,1)S(1)} %get-tuple-element.91), channel_id=1, source_target_pairs={{0,16},{1,17},{16,0},{17,1},{2,18},{3,19},{18,2},{19,3},{4,20},{5,... | collective-permute-start | bytes 393224 | tf_op jit(solution)/shard_map/ppermute | solution.py:29
  306.1 21.7 %collective-permute-start.58 = (bf16[4,128,1024]{2,1,0:T(8,128)(2,1)S(1)}, bf16[4,128,1024]{2,1,0:T(8,128)(2,1)S(1)}, u32[]{:S(2)}, u32[]{:S(2)}) collective-permute-start(bf16[4,128,1024]{2,1,0:T(8,128)(2,1)S(1)} %fusion.40), channel_id=1, source_target_pairs={{0,8},{8,0},{1,9},{9,1},{2,10},{10,2},{3,11},{11,3},{4,12},{12,4},... | collective-permute-start | bytes 3145736 | tf_op jit(solution)/shard_map/ppermute | solution.py:33
  315.0 15.4 %collective-permute-start.83 = (bf16[64,256]{1,0:T(8,128)(2,1)S(1)}, bf16[64,256]{1,0:T(8,128)(2,1)S(1)}, u32[]{:S(2)}, u32[]{:S(2)}) collective-permute-start(bf16[64,256]{1,0:T(8,128)(2,1)S(1)} %get-tuple-element.114), channel_id=1, source_target_pairs={{0,32},{32,64},{64,96},{96,0},{1,33},{33,65},{65,97},{97,1},{2,34}... | collective-permute-start | bytes 98312 | tf_op jit(solution)/shard_map/ppermute | solution.py:29
  315.1 16.6 %collective-permute-start.84 = (bf16[64,256]{1,0:T(8,128)(2,1)S(1)}, bf16[64,256]{1,0:T(8,128)(2,1)S(1)}, u32[]{:S(2)}, u32[]{:S(2)}) collective-permute-start(bf16[64,256]{1,0:T(8,128)(2,1)S(1)} %get-tuple-element.116), channel_id=1, source_target_pairs={{0,64},{32,96},{64,0},{96,32},{1,65},{33,97},{65,1},{97,33},{2,66}... | collective-permute-start | bytes 98312 | tf_op jit(solution)/shard_map/ppermute | solution.py:29
  335.9 15.5 %collective-permute-start.86 = (bf16[64,256]{1,0:T(8,128)(2,1)S(1)}, bf16[64,256]{1,0:T(8,128)(2,1)S(1)}, u32[]{:S(2)}, u32[]{:S(2)}) collective-permute-start(bf16[64,256]{1,0:T(8,128)(2,1)S(1)} %fusion.124), channel_id=1, source_target_pairs={{0,0},{1,8},{2,2},{3,10},{4,4},{5,12},{6,6},{7,14},{8,1},{9,9},{10... | collective-permute-start | bytes 98312 | tf_op jit(solution)/shard_map/ppermute | solution.py:42
  (84 other events, 690.9 us)
